TPU v7x, 512 devices: a whole 4x4x16 slice. The times are simulated.
512 devices in a mesh: seq: 128 (over z, y, core), ch: 4 (over x).
Axes of the slice: x: 4, y: 4, z: 16, core: 2. Of those that a mesh axis runs over, the one named last changes fastest.
Arguments:
- ingest: bfloat16 [131072, 4096], P('seq', 'ch'), may hold values from -6 to 6
- ingest_count: int32 [128], P('seq'), may hold values from 0 to 1024, as said below
- doc_lengths: int32 [128], replicated, may hold values from 1 to 2048, as said below
- in_weight: bfloat16 [4096, 5120], P('seq', 'ch'), may hold values from -0.09375 to 0.09375
- conv_weight: float32 [4, 5120], P(None, 'ch'), may hold values from -3 to 3
- conv_bias: float32 [5120], P('ch'), may hold values from -3 to 3
Outputs:
- conv_out: bfloat16 [65536, 5120], P('seq', 'ch')
Inputs may be any that keep to these rules, and one draw needn't show every extreme that they name: Device i keeps its valid rows in its first ingest_count[i] slots; the devices before i together hold between i * 512 - 256 and i * 512 + 256 rows, both ends reached in every draw; the first device holds 511 rows, and all devices together hold 65536 rows. `doc_lengths`: the lengths sum to 65536; the first document has exactly 2048 tokens.
All inputs are finite; a program needn't handle non-finite values.
Results may differ from a plain program's by a relative error of at most 0.012.
Values may be sent and summed in bfloat16 or wider, within the bound.
A program may use at most 128 MiB of HBM per device.

v0:
```python
import jax
import jax.numpy as jnp
from jax import lax
from jax.sharding import PartitionSpec as P


def shifted(value, axis, steps):
    count = lax.axis_size(axis)
    initial, last = (max(0, -steps), min(count, count - steps))
    return lax.ppermute(value, axis, [(source, source + steps) for source in range(initial, last)])


def carried_in(value, axis, join, neutral):
    count, mine = (lax.axis_size(axis), lax.axis_index(axis))
    pieces = lax.all_gather(value, axis)
    subtotal = jnp.full_like(value, 0) + jnp.asarray(neutral, value.dtype)

    def turn(position, subtotal):
        longer = join(subtotal, pieces[position])
        return jnp.where(position < mine, longer, subtotal)

    return lax.fori_loop(0, count - 1, turn, subtotal)


def move_rows(ingest, count, offset, first, tokens, extra):
    half = tokens // 2
    slots = ingest.shape[0]
    start = first + tokens - offset - extra
    tail = lax.dynamic_slice_in_dim(ingest, start, half + extra, 0)
    from_left = shifted(tail, "seq", 1)
    from_right = shifted(ingest[:half], "seq", -1)
    next_offset = offset + count
    buffer = jnp.concatenate([from_left, ingest, from_right], axis=0)
    places = first - extra + jnp.arange(tokens + extra, dtype=jnp.int32)
    lead = half + extra
    picks = jnp.where(
        places < offset,
        places - (first - extra),
        jnp.where(
            places < next_offset, lead + places - offset, lead + slots + places - next_offset
        ),
    )
    return jnp.take(buffer, picks.astype(jnp.int32), axis=0)


def body(ingest, ingest_count, doc_lengths, in_weight, conv_weight, conv_bias):
    tokens = ingest.shape[0] // 2
    channels = in_weight.shape[1]
    before = carried_in(
        ingest_count, "seq", lambda earlier, later: earlier + later, jnp.zeros_like(ingest_count)
    )
    offset = before[0]
    count = ingest_count[0]
    first = lax.axis_index("seq") * tokens
    extra = 3
    moved = move_rows(ingest, count, offset, first, tokens, extra)
    features = lax.all_gather(moved, "ch", axis=1, tiled=True)
    window = jnp.dot(
        features,
        lax.all_gather(in_weight, "seq", axis=0, tiled=True),
        preferred_element_type=jnp.float32,
    ).astype(jnp.bfloat16)
    values = window.astype(jnp.float32)
    starts = jnp.cumsum(doc_lengths) - doc_lengths
    places = first - 3 + jnp.arange(tokens + 3, dtype=jnp.int32)
    doc_ids = jnp.sum((places[:, None] >= starts[None, :]).astype(jnp.int32), axis=1) - 1
    here_ids = doc_ids[3:]
    total = jnp.zeros((tokens, channels), jnp.float32) + conv_bias[None, :]
    for lag in range(4):
        earlier = values[3 - lag : 3 - lag + tokens]
        same = (doc_ids[3 - lag : 3 - lag + tokens] == here_ids).astype(jnp.float32)
        total = total + conv_weight[lag][None, :] * earlier * same[:, None]
    return jax.nn.silu(total).astype(jnp.bfloat16)


def solution(mesh):
    placed = (P("seq", "ch"), P("seq"), P(), P("seq", "ch"), P(None, "ch"), P("ch"))
    return jax.shard_map(
        body, mesh=mesh, in_specs=placed, out_specs=P("seq", "ch"), check_vma=False
    )
```

profile of v0, /device:TPU:1, one launch (start us, length us, event | category | flops | bytes accessed | tf_op | source)
XLA Modules:
  0.0 486.9 jit_solution(12569060451620937295)
XLA Ops:
  7.2 1.3 dynamic-slice
  8.5 0.8 dynamic-update-slice
  9.2 30.5 %all-reduce = s32[128]{0:T(128)S(1)} all-reduce(s32[128]{0:T(128)S(1)} %dynamic-update-slice), channel_id=2, replica_groups=mesh['seq'=128,'ch'=4] {'seq'}, use_global_device_ids=true, to_apply=%add | all-reduce | flops 128 | bytes 1024
  39.7 175.2 %while.13 = (s32[]{:T(128)}, s32[1]{0:T(128)}, s32[]{:T(128)}, s32[128,1]{0,1:T(1,128)S(1)}, s32[]{:T(128)}) while((s32[]{:T(128)}, s32[1]{0:T(128)}, s32[]{:T(128)}, s32[128,1]{0,1:T(1,128)S(1)}, s32[]{:T(128)}) %tuple.40), condition=%wide.region_1.2_spmd, body=%wide.region_0.1_spmd.sunk | while | flops 5 | bytes 107 | solution.py:22
  41.1 0.7 constant_dynamic-slice_fusion.3
  42.5 0.7 constant_dynamic-slice_fusion.3
  43.9 0.7 constant_dynamic-slice_fusion.3
  45.3 0.7 constant_dynamic-slice_fusion.3
  46.6 0.7 constant_dynamic-slice_fusion.3
  48.0 0.7 constant_dynamic-slice_fusion.3
  49.4 0.7 constant_dynamic-slice_fusion.3
  50.8 0.7 constant_dynamic-slice_fusion.3
  52.2 0.7 constant_dynamic-slice_fusion.3
  53.5 0.7 constant_dynamic-slice_fusion.3
  54.9 0.7 constant_dynamic-slice_fusion.3
  56.3 0.7 constant_dynamic-slice_fusion.3
  57.7 0.7 constant_dynamic-slice_fusion.3
  59.1 0.7 constant_dynamic-slice_fusion.3
  215.0 1.2 constant_dynamic-slice_fusion.1
  216.2 7.4 %collective-permute-start = (bf16[259,1024]{1,0:T(8,128)(2,1)S(1)}, bf16[259,1024]{1,0:T(8,128)(2,1)}, u32[]{:S(2)}, u32[]{:S(2)}) collective-permute-start(bf16[259,1024]{1,0:T(8,128)(2,1)S(1)} %constant_dynamic-slice_fusion.1), channel_id=1, source_target_pairs={{0,4},{4,8},{8,12},{12,16},{16,20},{20,24},{24,28},{28,32},{32,36}... | collective-permute-start | bytes 1591304 | tf_op jit(solution)/shard_map/ppermute | solution.py:10
  223.6 1.1 slice.41
  224.7 2.2 collective-permute-start.1
  227.0 8.2 %collective-permute-done.1 = bf16[256,1024]{1,0:T(8,128)(2,1)S(1)} collective-permute-done((bf16[256,1024]{1,0:T(8,128)(2,1)S(1)}, bf16[256,1024]{1,0:T(8,128)(2,1)S(1)}, u32[]{:S(2)}, u32[]{:S(2)}) %collective-permute-start.1) | collective-permute-done | bytes 524320 | tf_op jit(solution)/shard_map/ppermute | solution.py:10
  235.2 0.8 copy-done
  236.0 14.8 %concatenate.3 = bf16[1539,1024]{1,0:T(8,128)(2,1)S(1)} concatenate(bf16[259,1024]{1,0:T(8,128)(2,1)} %collective-permute-done, bf16[1024,1024]{1,0:T(8,128)(2,1)} %param.8, bf16[256,1024]{1,0:T(8,128)(2,1)} %copy-done), dimensions={0} | concatenate | bytes 6303744 | tf_op jit(solution)/shard_map/concatenate | solution.py:33
  250.8 3.4 gather_fusion
  254.1 2.4 broadcast_select_fusion
  256.6 0.7 all-gather.6.cloned.1.call-update
  258.2 52.7 %all-gather.4.cloned.1.call-done = bf16[515,4096]{1,0:T(8,128)(2,1)} async-done(((bf16[515,1024]{1,0:T(8,128)(2,1)}), bf16[515,4096]{1,0:T(8,128)(2,1)}) %all-gather.4.cloned.1.call-update) | async-done | bytes 4218896 | tf_op jit(solution)/shard_map/all_gather | solution.py:57
  310.8 154.9 %all-gather.6.cloned.1.call-done = bf16[4096,1280]{1,0:T(8,128)(2,1)} async-done(((bf16[32,1280]{1,0:T(8,128)(2,1)}), bf16[4096,1280]{1,0:T(8,128)(2,1)}) %all-gather.6.cloned.1.call-update) | async-done | bytes 10485776 | tf_op jit(solution)/shard_map/all_gather | solution.py:60
  465.8 10.9 %fusion = f32[515,1280]{1,0:T(8,128)S(1)} fusion(bf16[515,4096]{1,0:T(8,128)(2,1)} %all-gather.4.cloned.1.call-done, bf16[4096,1280]{1,0:T(8,128)(2,1)} %all-gather.6.cloned.1.call-done), kind=kOutput, calls=%fused_computation.3 | convolution fusion | flops 5401485312 | bytes 17341440 | tf_op jit(solution)/shard_map/dot_general | solution.py:58
  476.7 3.3 multiply_convert_fusion
  (137 shorter events, 76.0 us)
Async XLA Ops:
  6.5 304.3 %all-gather.4.cloned.1.call-start = ((), (), s32[]{:S(2)}) async-start(), calls=%async_computation | async-start | bytes 5324800 | tf_op jit(solution)/shard_map/all_gather | solution.py:57
  216.2 19.8 %collective-permute-start = (bf16[259,1024]{1,0:T(8,128)(2,1)S(1)}, bf16[259,1024]{1,0:T(8,128)(2,1)}, u32[]{:S(2)}, u32[]{:S(2)}) collective-permute-start(bf16[259,1024]{1,0:T(8,128)(2,1)S(1)} %constant_dynamic-slice_fusion.1), channel_id=1, source_target_pairs={{0,4},{4,8},{8,12},{12,16},{16,20},{20,24},{24,28},{28,32},{32,36}... | collective-permute-start | bytes 1591304 | tf_op jit(solution)/shard_map/ppermute | solution.py:10
  224.7 10.5 %collective-permute-start.1 = (bf16[256,1024]{1,0:T(8,128)(2,1)S(1)}, bf16[256,1024]{1,0:T(8,128)(2,1)S(1)}, u32[]{:S(2)}, u32[]{:S(2)}) collective-permute-start(bf16[256,1024]{1,0:T(8,128)(2,1)S(1)} %slice.41), channel_id=1, source_target_pairs={{4,0},{8,4},{12,8},{16,12},{20,16},{24,20},{28,24},{32,28},{36,32}... | collective-permute-start | bytes 1572872 | tf_op jit(solution)/shard_map/ppermute | solution.py:10
  235.2 0.8 copy-start
  254.1 3.2 copy-start.3
  254.1 3.9 copy-start.1
  256.6 209.2 %all-gather.6.cloned.1.call-start = ((), (), s32[]{:S(2)}) async-start(), calls=%async_computation.1 | async-start | bytes 10567680 | tf_op jit(solution)/shard_map/all_gather | solution.py:60
  258.2 218.6 %copy-start.2 = (f32[1280]{0:T(1024)S(1)}, f32[1280]{0:T(1024)}, u32[]{:S(2)}) copy-start(f32[1280]{0:T(1024)} %param.13) | copy-start | bytes 15364
Sparse Core Ops, SparseCore 0:
  256.7 54.0 all-gather.3
  313.9 151.7 all-gather.5
where the time goes:
time: 489 us; the launch traced here: 487 us
  waiting for transfers between devices  217 us (44%)
  local copies, waits for them, and re-layouts  108 us (22%)
  loops' own time  90.8 us (19%)
  blocking collectives  30.5 us (6%)
  between operations  14.2 us (3%)
  matrix products  10.9 us (2%)
  starting transfers between devices  9.63 us (2%)
  other arithmetic  6.33 us (1%)
    all_gather x1, waiting for transfers between devices, body(): lax.all_gather(in_weight, 'seq', axis=0, tiled=True)  155 us
    another operation x1, loops' own time, carried_in(): return lax.fori_loop(0, count - 1, turn, subtotal)  90.8 us
    dynamic_slice x127, local copies, waits for them, and re-layouts, turn(): longer = join(subtotal, pieces[position])  84.4 us
    all_gather x1, waiting for transfers between devices, body(): features = lax.all_gather(moved, 'ch', axis=1, tiled=True)  52.7 us
    unnamed x1, blocking collectives  30.5 us
    concatenate x1, local copies, waits for them, and re-layouts, move_rows(): buffer = jnp.concatenate([from_left, ingest, from_right], axis=0)  14.8 us
    dot_general x1, matrix products, body(): jnp.dot(features, lax.all_gather(in_weight, 'seq', axis=0, tiled=True), p...  10.9 us
  transfers between devices with their start and end apart: 4, of which 3 were waited for; matrix products, arithmetic and copies ran while one was open for 0% of the time, Pallas kernels for 0%

commit v1 on v0

--- a/solution.py
+++ b/solution.py
@@ -44,6 +44,18 @@
 
 
 def body(ingest, ingest_count, doc_lengths, in_weight, conv_weight, conv_bias):
+
+    def widths_define(packet):
+        axis_total = jax.lax.axis_size("ch")
+        samples = [(b, (b + 1) % axis_total) for b in range(axis_total)]
+        z = [None] * axis_total
+        z[axis_total - 1] = packet
+        for ix in range(axis_total - 2, -1, -1):
+            z[ix] = jax.lax.ppermute(z[ix + 1], axis_name="ch", perm=samples)
+        h_now = jnp.concatenate(z, axis=1)
+        part_now = (jax.lax.axis_index("ch") + 1) * packet.shape[1]
+        return jnp.roll(h_now, part_now, axis=1)
+
     tokens = ingest.shape[0] // 2
     channels = in_weight.shape[1]
     before = carried_in(
@@ -54,7 +66,7 @@
     first = lax.axis_index("seq") * tokens
     extra = 3
     moved = move_rows(ingest, count, offset, first, tokens, extra)
-    features = lax.all_gather(moved, "ch", axis=1, tiled=True)
+    features = widths_define(moved)
     window = jnp.dot(
         features,
         lax.all_gather(in_weight, "seq", axis=0, tiled=True),

time: 489 us -> 339 us (0.69)
  the two profiles are of different devices: /device:TPU:1 before, /device:TPU:8 now
where the time goes in v1:
time: 339 us; the launch traced here: 337 us
  local copies, waits for them, and re-layouts  101 us (30%)
  waiting for transfers between devices  84 us (25%)
  loops' own time  72.9 us (22%)
  blocking collectives  33.3 us (10%)
  between operations  14.3 us (4%)
  starting transfers between devices  13.1 us (4%)
  matrix products  11 us (3%)
  other arithmetic  7.86 us (2%)
    ppermute x3, waiting for transfers between devices, widths_define(): z[ix] = jax.lax.ppermute(z[ix + 1], axis_name='ch', perm=samples)  76.7 us
    another operation x1, loops' own time, carried_in(): return lax.fori_loop(0, count - 1, turn, subtotal)  72.9 us
    dynamic_slice x127, local copies, waits for them, and re-layouts, turn(): longer = join(subtotal, pieces[position])  70.7 us
    unnamed x1, blocking collectives  33.3 us
    concatenate x1, local copies, waits for them, and re-layouts, move_rows(): buffer = jnp.concatenate([from_left, ingest, from_right], axis=0)  14.8 us
    dot_general x1, matrix products, body(): jnp.dot(features, lax.all_gather(in_weight, 'seq', axis=0, tiled=True), p...  11 us
    unnamed x19, local copies, waits for them, and re-layouts  9.25 us
    ppermute x3, starting transfers between devices, widths_define(): z[ix] = jax.lax.ppermute(z[ix + 1], axis_name='ch', perm=samples)  7.51 us
  transfers between devices with their start and end apart: 6, of which 4 were waited for; matrix products, arithmetic and copies ran while one was open for 31% of the time, Pallas kernels for 0%

profile of v1, /device:TPU:8, one launch (start us, length us, event | category | flops | bytes accessed | tf_op | source)
XLA Modules:
  0.0 336.9 jit_solution(3772194147720169817)
XLA Ops:
  6.5 0.7 all-gather.3.cloned.1.call-update
  7.9 1.2 dynamic-slice
  9.2 0.7 dynamic-update-slice
  9.8 33.3 %all-reduce = s32[128]{0:T(128)S(1)} all-reduce(s32[128]{0:T(128)S(1)} %dynamic-update-slice), channel_id=2, replica_groups=mesh['seq'=128,'ch'=4] {'seq'}, use_global_device_ids=true, to_apply=%add | all-reduce | flops 128 | bytes 1024
  43.1 143.6 %while.13 = (s32[]{:T(128)}, s32[1]{0:T(128)}, s32[]{:T(128)}, s32[128,1]{0,1:T(1,128)S(1)}, s32[]{:T(128)}) while((s32[]{:T(128)}, s32[1]{0:T(128)}, s32[]{:T(128)}, s32[128,1]{0,1:T(1,128)S(1)}, s32[]{:T(128)}) %tuple.38), condition=%wide.region_1.2_spmd, body=%wide.region_0.1_spmd.sunk | while | flops 5 | bytes 107 | solution.py:22
  46.5 0.6 constant_dynamic-slice_fusion.3
  49.9 0.6 constant_dynamic-slice_fusion.3
  186.7 1.2 constant_dynamic-slice_fusion.1
  187.9 1.9 collective-permute-start
  189.8 1.1 slice.41
  190.9 3.6 %collective-permute-start.1 = (bf16[256,1024]{1,0:T(8,128)(2,1)S(1)}, bf16[256,1024]{1,0:T(8,128)(2,1)S(1)}, u32[]{:S(2)}, u32[]{:S(2)}) collective-permute-start(bf16[256,1024]{1,0:T(8,128)(2,1)S(1)} %slice.41), channel_id=1, source_target_pairs={{4,0},{8,4},{12,8},{16,12},{20,16},{24,20},{28,24},{32,28},{36,32}... | collective-permute-start | bytes 1572872 | tf_op jit(solution)/shard_map/ppermute | solution.py:10
  194.6 6.6 %collective-permute-done.1 = bf16[256,1024]{1,0:T(8,128)(2,1)S(1)} collective-permute-done((bf16[256,1024]{1,0:T(8,128)(2,1)S(1)}, bf16[256,1024]{1,0:T(8,128)(2,1)S(1)}, u32[]{:S(2)}, u32[]{:S(2)}) %collective-permute-start.1) | collective-permute-done | bytes 524320 | tf_op jit(solution)/shard_map/ppermute | solution.py:10
  201.2 0.8 copy-done.1
  202.0 14.8 %concatenate.9 = bf16[1539,1024]{1,0:T(8,128)(2,1)S(1)} concatenate(bf16[259,1024]{1,0:T(8,128)(2,1)} %collective-permute-done, bf16[1024,1024]{1,0:T(8,128)(2,1)} %param.8, bf16[256,1024]{1,0:T(8,128)(2,1)} %copy-done.1), dimensions={0} | concatenate | bytes 6303744 | tf_op jit(solution)/shard_map/concatenate | solution.py:33
  216.9 3.4 gather_fusion
  220.2 1.4 broadcast_select_fusion
  221.6 3.4 %collective-permute-start.2 = (bf16[515,1024]{1,0:T(8,128)(2,1)S(1)}, bf16[515,1024]{1,0:T(8,128)(2,1)S(1)}, u32[]{:S(2)}, u32[]{:S(2)}) collective-permute-start(bf16[515,1024]{1,0:T(8,128)(2,1)S(1)} %broadcast_select_fusion), channel_id=1, source_target_pairs={{0,1},{1,2},{2,3},{3,0},{4,5},{5,6},{6,7},{7,4},{8,9},{9,10},{10,1... | collective-permute-start | bytes 3164168 | tf_op jit(solution)/shard_map/ppermute | solution.py:54
  225.1 25.8 %collective-permute-done.2 = bf16[515,1024]{1,0:T(8,128)(2,1)S(1)} collective-permute-done((bf16[515,1024]{1,0:T(8,128)(2,1)S(1)}, bf16[515,1024]{1,0:T(8,128)(2,1)S(1)}, u32[]{:S(2)}, u32[]{:S(2)}) %collective-permute-start.2) | collective-permute-done | bytes 1054752 | tf_op jit(solution)/shard_map/ppermute | solution.py:54
  250.9 2.2 collective-permute-start.3
  253.1 26.2 %collective-permute-done.3 = bf16[515,1024]{1,0:T(8,128)(2,1)S(1)} collective-permute-done((bf16[515,1024]{1,0:T(8,128)(2,1)S(1)}, bf16[515,1024]{1,0:T(8,128)(2,1)S(1)}, u32[]{:S(2)}, u32[]{:S(2)}) %collective-permute-start.3) | collective-permute-done | bytes 1054752 | tf_op jit(solution)/shard_map/ppermute | solution.py:54
  279.2 1.9 collective-permute-start.4
  282.0 24.7 %collective-permute-done.4 = bf16[515,1024]{1,0:T(8,128)(2,1)S(1)} collective-permute-done((bf16[515,1024]{1,0:T(8,128)(2,1)S(1)}, bf16[515,1024]{1,0:T(8,128)(2,1)S(1)}, u32[]{:S(2)}, u32[]{:S(2)}) %collective-permute-start.4) | collective-permute-done | bytes 1054752 | tf_op jit(solution)/shard_map/ppermute | solution.py:54
  306.7 1.1 constant_dynamic-update-slice_fusion.7
  307.8 1.1 constant_dynamic-update-slice_fusion.6
  308.9 1.1 constant_dynamic-update-slice_fusion.5
  310.0 1.3 constant_dynamic-update-slice_fusion.4
  311.3 1.1 constant_dynamic-update-slice_fusion.3
  312.3 1.1 constant_dynamic-update-slice_fusion.2
  313.5 1.1 constant_dynamic-update-slice_fusion.1
  314.5 1.3 constant_dynamic-update-slice_fusion
  315.8 11.0 %fusion.5 = f32[515,1280]{1,0:T(8,128)S(1)} fusion(bf16[4096,1280]{1,0:T(8,128)(2,1)} %all-gather.3.cloned.1.call-done, bf16[515,8192]{1,0:T(8,128)(2,1)} %constant_dynamic-update-slice_fusion, s32[]{:T(128)S(6)} %select_n.92), kind=kOutput, calls=%fused_computation.5 | convolution fusion | flops 5401485312 | bytes 17382404 | tf_op jit(solution)/shard_map/dot_general | solution.py:70
  326.8 3.3 multiply_convert_fusion
  (150 shorter events, 70.5 us)
Async XLA Ops:
  6.5 309.3 %all-gather.3.cloned.1.call-start = ((), (), s32[]{:S(2)}) async-start(), calls=%async_computation | async-start | bytes 10567680 | tf_op jit(solution)/shard_map/all_gather | solution.py:72
  187.9 14.1 %collective-permute-start = (bf16[259,1024]{1,0:T(8,128)(2,1)S(1)}, bf16[259,1024]{1,0:T(8,128)(2,1)}, u32[]{:S(2)}, u32[]{:S(2)}) collective-permute-start(bf16[259,1024]{1,0:T(8,128)(2,1)S(1)} %constant_dynamic-slice_fusion.1), channel_id=1, source_target_pairs={{0,4},{4,8},{8,12},{12,16},{16,20},{20,24},{24,28},{28,32},{32,36}... | collective-permute-start | bytes 1591304 | tf_op jit(solution)/shard_map/ppermute | solution.py:10
  190.9 10.3 %collective-permute-start.1 = (bf16[256,1024]{1,0:T(8,128)(2,1)S(1)}, bf16[256,1024]{1,0:T(8,128)(2,1)S(1)}, u32[]{:S(2)}, u32[]{:S(2)}) collective-permute-start(bf16[256,1024]{1,0:T(8,128)(2,1)S(1)} %slice.41), channel_id=1, source_target_pairs={{4,0},{8,4},{12,8},{16,12},{20,16},{24,20},{28,24},{32,28},{36,32}... | collective-permute-start | bytes 1572872 | tf_op jit(solution)/shard_map/ppermute | solution.py:10
  201.2 0.8 copy-start.1
  216.8 64.3 %copy-start.4 = (s32[128]{0:T(128)S(1)}, s32[128]{0:T(128)}, u32[]{:S(2)}) copy-start(s32[128]{0:T(128)} %param.10) | copy-start | bytes 1540
  216.9 65.0 %copy-start.2 = (f32[4,1280]{1,0:T(4,128)S(1)}, f32[4,1280]{1,0:T(4,128)}, u32[]{:S(2)}) copy-start(f32[4,1280]{1,0:T(4,128)} %param.12) | copy-start | bytes 61444
  221.6 29.2 %collective-permute-start.2 = (bf16[515,1024]{1,0:T(8,128)(2,1)S(1)}, bf16[515,1024]{1,0:T(8,128)(2,1)S(1)}, u32[]{:S(2)}, u32[]{:S(2)}) collective-permute-start(bf16[515,1024]{1,0:T(8,128)(2,1)S(1)} %broadcast_select_fusion), channel_id=1, source_target_pairs={{0,1},{1,2},{2,3},{3,0},{4,5},{5,6},{6,7},{7,4},{8,9},{9,10},{10,1... | collective-permute-start | bytes 3164168 | tf_op jit(solution)/shard_map/ppermute | solution.py:54
  250.9 28.4 %collective-permute-start.3 = (bf16[515,1024]{1,0:T(8,128)(2,1)S(1)}, bf16[515,1024]{1,0:T(8,128)(2,1)S(1)}, u32[]{:S(2)}, u32[]{:S(2)}) collective-permute-start(bf16[515,1024]{1,0:T(8,128)(2,1)S(1)} %collective-permute-done.2), channel_id=1, source_target_pairs={{0,1},{1,2},{2,3},{3,0},{4,5},{5,6},{6,7},{7,4},{8,9},{9,10},{10,1... | collective-permute-start | bytes 3164168 | tf_op jit(solution)/shard_map/ppermute | solution.py:54
  279.2 27.5 %collective-permute-start.4 = (bf16[515,1024]{1,0:T(8,128)(2,1)S(1)}, bf16[515,1024]{1,0:T(8,128)(2,1)S(1)}, u32[]{:S(2)}, u32[]{:S(2)}) collective-permute-start(bf16[515,1024]{1,0:T(8,128)(2,1)S(1)} %collective-permute-done.3), channel_id=1, source_target_pairs={{0,1},{1,2},{2,3},{3,0},{4,5},{5,6},{6,7},{7,4},{8,9},{9,10},{10,1... | collective-permute-start | bytes 3164168 | tf_op jit(solution)/shard_map/ppermute | solution.py:54
  307.8 2.2 copy-start
  315.8 11.0 %copy-start.3 = (f32[1280]{0:T(1024)S(1)}, f32[1280]{0:T(1024)}, u32[]{:S(2)}) copy-start(f32[1280]{0:T(1024)} %param.13) | copy-start | bytes 15364
Sparse Core Ops, SparseCore 0:
  10.5 152.7 all-gather.2
